TPU v7x, 32 devices: a whole 2x2x4 slice. The times are simulated.
32 devices in a mesh: rec: 2 (over y), tm: 4 (over z), chan: 4 (over x, core).
Axes of the slice: x: 2, y: 2, z: 4, core: 2. Of those that a mesh axis runs over, the one named last changes fastest.
Arguments:
- waveform: bfloat16 [204800], P(('rec', 'tm')), parts along dimension 0, may hold values from -56 to 56, as said below
- first_weight: bfloat16 [10, 512], P(None, 'chan'), may hold values from -2 to 2
- instance_gain: float32 [512], P('chan'), may hold values from 0.5 to 2
- instance_bias: float32 [512], P('chan'), may hold values from -3 to 3
- second_weight: bfloat16 [3, 512, 512], P(None, None, 'chan'), may hold values from -0.15625 to 0.15625
- third_weight: bfloat16 [3, 512, 512], P(None, None, 'chan'), may hold values from -0.15625 to 0.15625
- feature_gain: float32 [512], replicated, may hold values from 0.5 to 2
- feature_bias: float32 [512], replicated, may hold values from -3 to 3
- project_weight: bfloat16 [512, 1024], P(None, 'chan'), may hold values from -0.25 to 0.25
- project_bias: float32 [1024], replicated, may hold values from -3 to 3
- position_weight: bfloat16 [1024, 8192], P('chan'), may hold values from -0.0625 to 0.0625
- position_bias: float32 [1024], P('chan'), may hold values from -3 to 3
- final_gain: float32 [1024], P('chan'), may hold values from 0.5 to 2
- final_bias: float32 [1024], P('chan'), may hold values from -3 to 3
Outputs:
- encoded: bfloat16 [1024, 10240], P('chan', ('rec', 'tm')), parts along dimension 1
There are 2 independent parts, one for each index of `rec`. A program takes and returns all parts, laid end to end along the dimension named above; an argument that names none is the same for every part. Nothing has to cross between parts.
Inputs may be any that keep to these rules, and one draw needn't show every extreme that they name: `waveform`: samples of one recording.
All inputs are finite; a program needn't handle non-finite values.
Results may differ from a plain program's by a relative error of at most 0.005.
The roundings to bfloat16 on the way count: a program that leaves them out, or rounds other values in their place, can miss the bound.
Values may be sent and summed in bfloat16 or wider, within the bound.
A program may use at most 128 MiB of HBM per device.

v0:
```python
import functools

import jax
import jax.numpy as jnp
from jax import lax
from jax.experimental import pallas as pl
from jax.experimental.pallas import tpu as pltpu
from jax.sharding import PartitionSpec as P

K = 128
GW = 64
HALF = K // 2
SPAN = 32
PHASES = K // SPAN
MESH = pl.DeviceIdType.MESH
NT = (((1,), (1,)), ((), ()))


def gelu_exact(values):
    return 0.5 * values * (1.0 + lax.erf(values * 0.7071067811865476))


def rows_per_device(frames, count):
    return -(-(frames + K) // (16 * count)) * 16


def shifted(value, axis, steps):
    count = lax.axis_size(axis)
    leading, last = (max(0, -steps), min(count, count - steps))
    return lax.ppermute(value, axis, [(source, source + steps) for source in range(leading, last)])


def tail_kernel(
    n,
    frames,
    rows,
    model_width,
    normed,
    project_weight,
    params,
    position_weight,
    out,
    gathered,
    taps,
    x32,
    x2,
    window,
    partial,
    positional,
    summed,
    stats,
    taps_sem,
    send_sem,
    recv_sem,
    pair_send,
    pair_recv,
    stat_send,
    stat_recv,
):
    me = lax.axis_index("chan")
    shard = lax.axis_index("tm")
    shards = lax.axis_size("tm")
    chips = n // 2
    chip, core = me // 2, lax.rem(me, 2)
    pair = chip * 2 + 1 - core
    width = out.shape[0]
    groups = width // GW

    barrier = pltpu.get_barrier_semaphore()
    for step in range(1, n):
        pl.semaphore_signal(
            barrier, inc=1, device_id={"chan": lax.rem(me + step, n)}, device_id_type=MESH
        )

    tap_copies = []
    for g in range(groups):
        for p in range(PHASES):
            copy = pltpu.make_async_copy(
                position_weight.at[pl.ds(g * GW, GW), pl.ds(p * SPAN * GW, SPAN * GW)],
                taps.at[g, pl.ds(p * GW, GW), :],
                taps_sem.at[g, p],
            )
            copy.start()
            tap_copies.append(copy)

    pl.semaphore_wait(barrier, n - 1)

    def block(index):
        return gathered.at[pl.ds(pl.multiple_of(index * rows, 16), rows), :]

    chip_copies = []
    for step in range(1, chips):
        copy = pltpu.make_async_remote_copy(
            src_ref=normed,
            dst_ref=block(me),
            send_sem=send_sem.at[step],
            recv_sem=recv_sem.at[step],
            device_id={"chan": lax.rem(chip + step, chips) * 2 + core},
            device_id_type=MESH,
        )
        copy.start()
        chip_copies.append(copy)
    first_pair = pltpu.make_async_remote_copy(
        src_ref=normed,
        dst_ref=block(me),
        send_sem=pair_send.at[0],
        recv_sem=pair_recv.at[0],
        device_id={"chan": pair},
        device_id_type=MESH,
    )
    first_pair.start()

    def project(index, source):
        values = jnp.dot(source[...], project_weight[...], preferred_element_type=jnp.float32)
        values = (values + params[0:1, :]).astype(jnp.bfloat16).astype(jnp.float32)
        frame = (
            shard * frames
            - HALF
            + index * rows
            + lax.broadcasted_iota(jnp.int32, (rows, 1), 0)
        )
        inside = (frame >= 0) & (frame < shards * frames)
        x32[pl.ds(pl.multiple_of(index * rows, 8), rows), :] = jnp.where(inside, values, 0.0)

    x32[n * rows :, :] = jnp.zeros_like(x32[n * rows :, :])
    x2[...] = jnp.zeros_like(x2)
    project(me, normed)
    first_pair.wait_recv()
    project(pair, block(pair))
    forwards = []
    for step in range(1, chips):
        other = lax.rem(chip + chips - step, chips) * 2 + core
        chip_copies[step - 1].wait_recv()
        copy = pltpu.make_async_remote_copy(
            src_ref=block(other),
            dst_ref=block(other),
            send_sem=pair_send.at[step],
            recv_sem=pair_recv.at[step],
            device_id={"chan": pair},
            device_id_type=MESH,
        )
        copy.start()
        forwards.append(copy)
        project(other, block(other))
    for step in range(1, chips):
        other = lax.rem(chip + chips - step, chips) * 2 + 1 - core
        forwards[step - 1].wait_recv()
        project(other, block(other))

    length = frames + K
    chunk = length // 4
    for g in range(groups):
        lanes = slice(g * GW, (g + 1) * GW)
        x2[0:length, :] = jnp.concatenate(
            [x32[0:length, lanes], x32[1 : length + 1, lanes]], axis=1
        )
        for q in range(SPAN // 4):
            window[:, q * 2 * GW : (q + 1) * 2 * GW] = x2[
                2 * q : 2 * q + length + 16, :
            ].astype(jnp.bfloat16)
        for p in range(PHASES):
            tap_copies[g * PHASES + p].wait()
        middle = SPAN // 2 * GW

        @pl.loop(0, 4)
        def _(m):
            start = pl.multiple_of(m * chunk, 16)
            partial[pl.ds(start, chunk), :] = lax.dot_general(
                window[pl.ds(start, chunk), :],
                taps[g, :, 0:middle],
                NT,
                preferred_element_type=jnp.float32,
            ) + lax.dot_general(
                window[pl.ds(pl.multiple_of(start + 16, 16), chunk), :],
                taps[g, :, middle : 2 * middle],
                NT,
                preferred_element_type=jnp.float32,
            )

        total = partial[0:frames, 0:GW]
        for p in range(1, PHASES):
            total = total + partial[p * SPAN : p * SPAN + frames, p * GW : (p + 1) * GW]
        positional[:, lanes] = total

    tile = 128

    @pl.loop(0, frames // tile)
    def _(m):
        start = pl.multiple_of(m * tile, tile)
        values = x32[pl.ds(start + HALF, tile), :] + gelu_exact(
            positional[pl.ds(start, tile), :] + params[1:2, :]
        )
        turned = values.T
        summed[:, pl.ds(start, tile)] = turned
        stats[me, 0:1, pl.ds(start, tile)] = jnp.sum(turned, axis=0, keepdims=True)
        stats[me, 1:2, pl.ds(start, tile)] = jnp.sum(turned * turned, axis=0, keepdims=True)

    stat_copies = []
    for step in range(1, n):
        copy = pltpu.make_async_remote_copy(
            src_ref=stats.at[me],
            dst_ref=stats.at[me],
            send_sem=stat_send.at[step],
            recv_sem=stat_recv.at[step],
            device_id={"chan": lax.rem(me + step, n)},
            device_id_type=MESH,
        )
        copy.start()
        stat_copies.append(copy)
    gain_bias = params[...].T
    for copy in stat_copies:
        copy.wait_recv()
    gain, bias = gain_bias[:, 2:3], gain_bias[:, 3:4]

    @pl.loop(0, frames // tile)
    def _(m):
        start = pl.multiple_of(m * tile, tile)
        both = stats[0, 0:2, pl.ds(start, tile)]
        for index in range(1, n):
            both = both + stats[index, 0:2, pl.ds(start, tile)]
        mean = both[0:1] / model_width
        scale = lax.rsqrt(both[1:2] / model_width - mean * mean + 1e-05)
        out[:, pl.ds(start, tile)] = (
            (summed[:, pl.ds(start, tile)] - mean) * scale * gain + bias
        ).astype(jnp.bfloat16)

    for copy in chip_copies + [first_pair] + forwards + stat_copies:
        copy.wait_send()


def tail(normed, project_weight, params, position_weight, n, frames, model_width):
    rows, channels = normed.shape
    width = project_weight.shape[1]
    groups = width // GW
    length = frames + K
    vmem = pl.BlockSpec(memory_space=pltpu.VMEM)
    dma = pltpu.SemaphoreType.DMA
    return pl.pallas_call(
        functools.partial(tail_kernel, n, frames, rows, model_width),
        out_shape=jax.ShapeDtypeStruct((width, frames), jnp.bfloat16),
        in_specs=[vmem, vmem, vmem, pl.BlockSpec(memory_space=pl.ANY)],
        out_specs=vmem,
        scratch_shapes=[
            pltpu.VMEM((n * rows, channels), jnp.bfloat16),
            pltpu.VMEM((groups, PHASES * GW, SPAN * GW), jnp.bfloat16),
            pltpu.VMEM((n * rows + 64, width), jnp.float32),
            pltpu.VMEM((length + 64, 2 * GW), jnp.float32),
            pltpu.VMEM((length + 16, SPAN // 2 * GW), jnp.bfloat16),
            pltpu.VMEM((length, PHASES * GW), jnp.float32),
            pltpu.VMEM((frames, width), jnp.float32),
            pltpu.VMEM((width, frames), jnp.float32),
            pltpu.VMEM((n, 2, frames), jnp.float32),
            dma((groups, PHASES)),
            dma((n // 2,)),
            dma((n // 2,)),
            dma((n // 2,)),
            dma((n // 2,)),
            dma((n,)),
            dma((n,)),
        ],
        compiler_params=pltpu.CompilerParams(
            collective_id=0, has_side_effects=True, vmem_limit_bytes=48 * 1024 * 1024
        ),
        name="tail",
    )(normed, project_weight, params, position_weight)


def feature_norm(rows, gain, bias):
    values = rows.astype(jnp.float32)
    mean = jnp.mean(values, axis=1, keepdims=True)
    centred = values - mean
    spread = jnp.mean(centred * centred, axis=1, keepdims=True)
    return (centred * lax.rsqrt(spread + 1e-05) * gain + bias).astype(jnp.bfloat16)


def local(
    waveform,
    first_weight,
    instance_gain,
    instance_bias,
    second_weight,
    third_weight,
    feature_gain,
    feature_bias,
    project_weight,
    project_bias,
    position_weight,
    position_bias,
    final_gain,
    final_bias,
):
    n = lax.axis_size("chan")
    me = lax.axis_index("chan")
    shards = lax.axis_size("tm")
    shard = lax.axis_index("tm")
    frames = waveform.shape[0] // 20
    rows = rows_per_device(frames, n)
    channels = feature_gain.shape[0]
    width = project_weight.shape[1]
    model_width = width * n

    weights = lax.all_gather(
        jnp.concatenate([second_weight, third_weight], 0), "chan", axis=2, tiled=True
    )
    second_full = weights[:3].reshape(3 * channels, channels)
    third_full = weights[3:].reshape(3 * channels, channels)
    small = lax.all_gather(
        jnp.concatenate(
            [first_weight.astype(jnp.float32), instance_gain[None], instance_bias[None]], 0
        ),
        "chan",
        axis=1,
        tiled=True,
    )
    first_full = small[:10].astype(jnp.bfloat16)
    gain, offset = small[10], small[11]

    after = 20 * (n * rows - HALF - frames) + 40
    before = 20 * HALF
    samples = jnp.concatenate(
        [shifted(waveform[-before:], "tm", 1), waveform, shifted(waveform[:after], "tm", -1)]
    )
    mine = lax.dynamic_slice_in_dim(samples, me * rows * 20, (rows + 2) * 20)
    mine = mine.reshape(rows + 2, 20)
    patches = jnp.concatenate([mine[:-1], mine[1:, :5]], axis=1)
    band = jnp.concatenate(
        [jnp.pad(first_full, ((5 * f, 15 - 5 * f), (0, 0))) for f in range(4)], axis=1
    )
    conv = jnp.dot(patches, band, preferred_element_type=jnp.float32)
    place = me * rows - HALF + jnp.arange(rows + 1)[:, None]
    counted = (place >= 0) & (place < frames) & (jnp.arange(rows + 1)[:, None] < rows)
    kept = jnp.where(counted, conv, 0.0)
    sums = jnp.stack([jnp.sum(kept, axis=0), jnp.sum(kept * kept, axis=0)])
    sums = jnp.sum(sums.reshape(2, 4, channels), axis=1)
    sums = lax.psum(sums, ("tm", "chan"))
    count = 4 * frames * shards
    mean_first = sums[0] / count
    var_first = sums[1] / count - mean_first * mean_first
    scale = lax.rsqrt(var_first + 1e-05)
    spread = [jnp.tile(v, 4) for v in (mean_first, scale, gain, offset)]
    first = gelu_exact((conv - spread[0]) * spread[1] * spread[2] + spread[3])
    inside = (shard * frames + place >= 0) & (shard * frames + place < shards * frames)
    first = jnp.where(inside, first, 0.0).astype(jnp.bfloat16)

    def dot(a, b):
        return jnp.dot(a, b, preferred_element_type=jnp.float32)

    c = channels
    second_even = gelu_exact(dot(first[:, : 3 * c], second_full)).astype(jnp.bfloat16)
    second_odd = gelu_exact(
        dot(first[:-1, 2 * c :], second_full[: 2 * c]) + dot(first[1:, :c], second_full[2 * c :])
    ).astype(jnp.bfloat16)
    third = gelu_exact(
        dot(second_even[:-1], third_full[:c])
        + dot(second_odd, third_full[c : 2 * c])
        + dot(second_even[1:], third_full[2 * c :])
    ).astype(jnp.bfloat16)
    normed = feature_norm(third, feature_gain, feature_bias)

    bias_here = lax.dynamic_slice_in_dim(project_bias, me * width, width)
    params = jnp.stack([bias_here, position_bias, final_gain, final_bias])
    params = jnp.pad(params, ((0, 4), (0, 0)))
    return tail(normed, project_weight, params, position_weight, n, frames, model_width)


def solution(mesh):
    return jax.shard_map(
        local,
        mesh=mesh,
        in_specs=(
            P(("rec", "tm")),
            P(None, "chan"),
            P("chan"),
            P("chan"),
            P(None, None, "chan"),
            P(None, None, "chan"),
            P(),
            P(),
            P(None, "chan"),
            P(),
            P("chan", None),
            P("chan"),
            P("chan"),
            P("chan"),
        ),
        out_specs=P("chan", ("rec", "tm")),
        check_vma=False,
    )
```

profile of v0, /device:TPU:0, one launch (start us, length us, event | category | flops | bytes accessed | tf_op | source)
XLA Modules:
  0.0 117.6 jit_solution(1566747245759740397)
XLA Ops:
  6.5 0.0 all-gather.2.cloned.1.call-start
  6.5 2.1 %pad_maximum_fusion = bf16[6,512,128]{2,1,0:T(8,128)(2,1)} fusion(bf16[3,512,128]{2,1,0:T(8,128)(2,1)} %param.19, bf16[3,512,128]{2,1,0:T(8,128)(2,1)} %param.18), kind=kLoop, calls=%fused_computation.12 | loop fusion | flops 393216 | bytes 1572864 | tf_op jit(solution)/shard_map/concatenate | solution.py:303
  8.6 0.0 all-gather.2.cloned.1.call-update
  8.6 0.7 slice.93
  9.3 4.9 %collective-permute-start = (bf16[1280]{0:T(1024)(128)(2,1)S(1)}, bf16[1280]{0:T(1024)(128)(2,1)S(1)}, u32[]{:S(2)}, u32[]{:S(2)}) collective-permute-start(bf16[1280]{0:T(1024)(128)(2,1)S(1)} %slice.93), channel_id=1, source_target_pairs={{0,4},{4,8},{8,12},{1,5},{5,9},{9,13},{2,6},{6,10},{10,14},{3,7},{... | collective-permute-start | bytes 7688 | tf_op jit(solution)/shard_map/ppermute | solution.py:30
  14.3 0.7 slice.94
  14.9 1.3 %collective-permute-start.1 = (bf16[1320]{0:T(1024)(128)(2,1)S(1)}, bf16[1320]{0:T(1024)(128)(2,1)S(1)}, u32[]{:S(2)}, u32[]{:S(2)}) collective-permute-start(bf16[1320]{0:T(1024)(128)(2,1)S(1)} %slice.94), channel_id=1, source_target_pairs={{4,0},{8,4},{12,8},{5,1},{9,5},{13,9},{6,2},{10,6},{14,10},{7,3},{... | collective-permute-start | bytes 7928 | tf_op jit(solution)/shard_map/ppermute | solution.py:30
  16.2 0.7 convert_element_type.32
  16.9 0.8 dynamic_slice.7
  17.7 0.7 pad_maximum_fusion.1
  18.4 5.2 %all_gather.6 = f32[12,512]{1,0:T(8,128)S(1)} all-gather(f32[12,128]{1,0:T(8,128)S(1)} %pad_maximum_fusion.1), channel_id=1, replica_groups=mesh['rec'=2,'tm'=4,'chan'=4] {'chan'}, dimensions={1}, use_global_device_ids=true | all-gather | bytes 30720 | tf_op jit(solution)/shard_map/all_gather | solution.py:307
  23.6 0.7 select_maximum_fusion.params
  24.4 0.0 collective-permute-done
  24.4 0.0 collective-permute-done.1
  24.4 0.9 fusion.46
  25.3 0.2 reshape.70
  25.5 0.1 copy.18
  25.6 0.3 slice.96
  25.9 0.1 copy.17
  26.0 0.7 select_reduce_fusion
  26.7 35.2 %psum.7 = f32[2,512]{1,0:T(2,128)S(1)} all-reduce(f32[2,512]{1,0:T(2,128)S(1)} %maximum_reduce_fusion), channel_id=1, replica_groups=mesh['rec'=2,'tm'=4,'chan'=4] {'tm','chan'}, use_global_device_ids=true, to_apply=%region_3.4 | all-reduce | flops 1024 | bytes 8192 | tf_op jit(solution)/shard_map/psum | solution.py:335
  62.0 2.1 %select_convert_fusion = bf16[353,2048]{1,0:T(8,128)(2,1)} fusion(f32[353,2048]{1,0:T(8,128)S(1)} %get-tuple-element.11, f32[2048]{0:T(1024)S(1)} %bitcast.46, f32[2048]{0:T(1024)S(1)} %bitcast.45, f32[2048]{0:T(1024)S(1)} %bitcast.48, f32[2048]{0:T(1024)S(1)} %bitcast.47, pred[353]{0:T(512)(128)(4,1)S(1)} %fusion.53), kind=kLoop, calls=%fused_computation | loop fusion | flops 7229440 | bytes 4370785 | tf_op jit(solution)/shard_map/convert_element_type | solution.py:343
  64.1 0.0 all-gather.2.cloned.1.call-done
  64.1 1.3 %slice.131 = bf16[2,512,512]{2,1,0:T(8,128)(2,1)S(1)} slice(bf16[6,512,512]{2,1,0:T(8,128)(2,1)} %all-gather.2.cloned.1.call-done), slice={[0:2], [0:512], [0:512]} | slice | bytes 2097152 | tf_op jit(solution)/shard_map/slice | solution.py:351
  65.4 0.0 slice-start
  65.5 0.0 copy-start.4
  65.5 2.7 %fusion.10 = f32[352,512]{1,0:T(8,128)} fusion(bf16[1024,512]{1,0:T(8,128)(2,1)S(1)} %bitcast.43, bf16[353,2048]{1,0:T(8,128)(2,1)} %select_convert_fusion), kind=kOutput, calls=%fused_computation.18 | convolution fusion | flops 369098752 | bytes 2490368 | tf_op jit(solution)/shard_map/dot_general | solution.py:346
  68.1 0.0 slice-done
  68.1 0.0 copy-done.4
  68.1 0.0 copy-start.2
  68.1 0.8 multiply_convert_fusion
  68.9 0.0 copy-start.5
  68.9 0.7 copy-done.5
  69.7 0.5 copy-done.2
  70.2 0.0 copy-start.3
  70.2 1.3 %fusion.12 = f32[352,512]{1,0:T(8,128)} fusion(bf16[6,512,512]{2,1,0:T(8,128)(2,1)S(1)} %copy-done.2, bf16[353,512]{1,0:T(8,128)(2,1)S(1)} %multiply_convert_fusion), kind=kOutput, calls=%fused_computation.26 | convolution fusion | flops 184549376 | bytes 1605632 | tf_op jit(solution)/shard_map/dot_general | solution.py:346
  71.4 3.4 %convolution_add_fusion.1 = f32[352,512]{1,0:T(8,128)} fusion(f32[352,512]{1,0:T(8,128)} %fusion.12, f32[352,512]{1,0:T(8,128)} %fusion.10, bf16[6,512,512]{2,1,0:T(8,128)(2,1)} %all-gather.2.cloned.1.call-done, bf16[353,2048]{1,0:T(8,128)(2,1)} %select_convert_fusion), kind=kOutput, calls=%fused_computation.4 | convolution fusion | flops 370360320 | bytes 3571712 | tf_op jit(solution)/shard_map/dot_general | solution.py:346
  74.8 0.0 copy-done.3
  74.8 1.8 %convert_reduce_fusion = (f32[352]{0:T(512)S(1)}, bf16[352,512]{1,0:T(8,128)(2,1)S(1)}) fusion(f32[352,512]{1,0:T(8,128)} %convolution_add_fusion.1, bf16[6,512,512]{2,1,0:T(8,128)(2,1)S(1)} %copy-done.3, bf16[353,512]{1,0:T(8,128)(2,1)} %copy-done.5), kind=kOutput, calls=%fused_computation.9 | convolution fusion | flops 185990816 | bytes 1967488 | tf_op jit(solution)/shard_map/dot_general | solution.py:346
  76.6 0.3 fusion.6
  76.8 0.0 copy-done.6
  76.8 0.0 copy-done.7
  76.8 0.2 fusion.9.normed
  77.1 0.0 copy-done.1
  77.1 0.0 copy-start
  77.1 2.2 %copy-done = bf16[256,8192]{1,0:T(8,128)(2,1)S(1)} copy-done((bf16[256,8192]{1,0:T(8,128)(2,1)S(1)}, bf16[256,8192]{1,0:T(8,128)(2,1)}, u32[]{:S(2)}) %copy-start) | copy-done | bytes 4194328
  79.3 30.7 %tail.1 = bf16[256,1280]{1,0:T(8,128)(2,1)S(1)} custom-call(bf16[352,512]{1,0:T(8,128)(2,1)S(1)} %fusion.9.normed, bf16[512,256]{1,0:T(8,128)(2,1)S(1)} %copy-done.1, f32[8,256]{1,0:T(8,128)S(1)} %select_maximum_fusion.params, bf16[256,8192]{1,0:T(8,128)(2,1)S(1)} %copy-done), custom_call_target="tpu_custom_call" | custom-call | tf_op jit(solution)/shard_map/tail/pallas_call | solution.py:238
  109.9 0.8 copy.24
  (22 shorter events, 0.2 us)
Async XLA Ops:
  6.5 57.6 %all-gather.2.cloned.1.call-start = ((), (), s32[]{:S(2)}) async-start(), calls=%async_computation | async-start | bytes 3932160 | tf_op jit(solution)/shard_map/all_gather | solution.py:302
  9.3 15.1 %collective-permute-start = (bf16[1280]{0:T(1024)(128)(2,1)S(1)}, bf16[1280]{0:T(1024)(128)(2,1)S(1)}, u32[]{:S(2)}, u32[]{:S(2)}) collective-permute-start(bf16[1280]{0:T(1024)(128)(2,1)S(1)} %slice.93), channel_id=1, source_target_pairs={{0,4},{4,8},{8,12},{1,5},{5,9},{9,13},{2,6},{6,10},{10,14},{3,7},{... | collective-permute-start | bytes 7688 | tf_op jit(solution)/shard_map/ppermute | solution.py:30
  14.9 9.5 %collective-permute-start.1 = (bf16[1320]{0:T(1024)(128)(2,1)S(1)}, bf16[1320]{0:T(1024)(128)(2,1)S(1)}, u32[]{:S(2)}, u32[]{:S(2)}) collective-permute-start(bf16[1320]{0:T(1024)(128)(2,1)S(1)} %slice.94), channel_id=1, source_target_pairs={{4,0},{8,4},{12,8},{5,1},{9,5},{13,9},{6,2},{10,6},{14,10},{7,3},{... | collective-permute-start | bytes 7928 | tf_op jit(solution)/shard_map/ppermute | solution.py:30
  65.4 2.7 %slice-start = ((bf16[6,512,512]{2,1,0:T(8,128)(2,1)}), bf16[3,512,512]{2,1,0:T(8,128)(2,1)S(1)}, s32[]{:S(2)}) async-start(bf16[6,512,512]{2,1,0:T(8,128)(2,1)} %all-gather.2.cloned.1.call-done), calls=%async_computation.1 | async-start | bytes 3145728 | tf_op jit(solution)/shard_map/slice | solution.py:305
  65.5 2.7 %copy-start.4 = (bf16[353,2048]{1,0:T(8,128)(2,1)S(1)}, bf16[353,2048]{1,0:T(8,128)(2,1)}, u32[]{:S(2)}) copy-start(bf16[353,2048]{1,0:T(8,128)(2,1)} %select_convert_fusion) | copy-start | bytes 4337668
  68.1 2.0 %copy-start.2 = (bf16[6,512,512]{2,1,0:T(8,128)(2,1)S(1)}, bf16[6,512,512]{2,1,0:T(8,128)(2,1)}, u32[]{:S(2)}) copy-start(bf16[6,512,512]{2,1,0:T(8,128)(2,1)} %all-gather.2.cloned.1.call-done) | copy-start | bytes 9437188
  68.9 0.7 copy-start.5
  70.2 4.6 %copy-start.3 = (bf16[6,512,512]{2,1,0:T(8,128)(2,1)S(1)}, bf16[6,512,512]{2,1,0:T(8,128)(2,1)}, u32[]{:S(2)}) copy-start(bf16[6,512,512]{2,1,0:T(8,128)(2,1)} %all-gather.2.cloned.1.call-done) | copy-start | bytes 9437188
  71.4 5.4 %copy-start.6 = (f32[512]{0:T(512)S(1)}, f32[512]{0:T(512)}, u32[]{:S(2)}) copy-start(f32[512]{0:T(512)} %param.21) | copy-start | bytes 6148
  71.4 5.4 %copy-start.7 = (f32[512]{0:T(512)S(1)}, f32[512]{0:T(512)}, u32[]{:S(2)}) copy-start(f32[512]{0:T(512)} %param.20) | copy-start | bytes 6148
  71.4 5.6 %copy-start.1 = (bf16[512,256]{1,0:T(8,128)(2,1)S(1)}, bf16[512,256]{1,0:T(8,128)(2,1)}, u32[]{:S(2)}) copy-start(bf16[512,256]{1,0:T(8,128)(2,1)} %project_weight.1) | copy-start | bytes 786436
  77.1 2.2 %copy-start = (bf16[256,8192]{1,0:T(8,128)(2,1)S(1)}, bf16[256,8192]{1,0:T(8,128)(2,1)}, u32[]{:S(2)}) copy-start(bf16[256,8192]{1,0:T(8,128)(2,1)} %position_weight.1) | copy-start | bytes 12582916
Sparse Core Ops, SparseCore 0:
  8.9 31.9 all-gather.1
where the time goes:
time: 118 us
  blocking collectives  40.4 us (34%)
  Pallas kernels  30.7 us (26%)
  between operations  13.7 us (12%)
  matrix products  10.5 us (9%)
  local copies, waits for them, and re-layouts  8.45 us (7%)
  other arithmetic  7.69 us (7%)
  starting transfers between devices  6.2 us (5%)
    psum x1, blocking collectives, local(): sums = lax.psum(sums, ('tm', 'chan'))  35.2 us
    pallas_call x1, Pallas kernels, tail(): pl.pallas_call(functools.partial(tail_kernel, n, frames, rows, model_widt...  30.7 us
    dot_general x5, matrix products, dot(): return jnp.dot(a, b, preferred_element_type=jnp.float32)  9.82 us
    ppermute x2, starting transfers between devices, shifted(): lax.ppermute(value, axis, [(source, source + steps) for source in range(l...  6.2 us
    all_gather x1, blocking collectives, local(): lax.all_gather(jnp.concatenate([first_weight.astype(jnp.float32), instanc...  5.18 us
    unnamed x25, local copies, waits for them, and re-layouts  4.28 us
  transfers between devices with their start and end apart: 3, of which 0 were waited for; matrix products, arithmetic and copies ran while one was open for 7% of the time, Pallas kernels for 0%

commit v1 on v0

--- a/solution.py
+++ b/solution.py
@@ -24,22 +24,35 @@
     return -(-(frames + K) // (16 * count)) * 16
 
 
-def shifted(value, axis, steps):
-    count = lax.axis_size(axis)
-    leading, last = (max(0, -steps), min(count, count - steps))
-    return lax.ppermute(value, axis, [(source, source + steps) for source in range(leading, last)])
-
-
-def tail_kernel(
+def encoder_kernel(
     n,
+    shards,
     frames,
     rows,
     model_width,
-    normed,
+    waveform,
+    small,
+    second_weight,
+    third_weight,
+    feature,
     project_weight,
     params,
     position_weight,
     out,
+    samples,
+    sample32,
+    smalls,
+    band32,
+    conv,
+    first,
+    shift32,
+    second,
+    slots,
+    full,
+    own_stats,
+    chan_stats,
+    tm_stats,
+    normed,
     gathered,
     taps,
     x32,
@@ -49,6 +62,19 @@
     positional,
     summed,
     stats,
+    own_sem,
+    halo_send,
+    halo_recv,
+    small_send,
+    small_recv,
+    weight_send,
+    weight_recv,
+    weight_pair_send,
+    weight_pair_recv,
+    moment_send,
+    moment_recv,
+    total_send,
+    total_recv,
     taps_sem,
     send_sem,
     recv_sem,
@@ -59,18 +85,116 @@
 ):
     me = lax.axis_index("chan")
     shard = lax.axis_index("tm")
-    shards = lax.axis_size("tm")
     chips = n // 2
     chip, core = me // 2, lax.rem(me, 2)
     pair = chip * 2 + 1 - core
     width = out.shape[0]
     groups = width // GW
+    channels = feature.shape[1]
+    part = channels // n
+    after = samples.shape[0] - HALF - frames
+    sent = []
+
+    def send(source, target, send_at, recv_at, **device):
+        copy = pltpu.make_async_remote_copy(
+            src_ref=source,
+            dst_ref=target,
+            send_sem=send_at,
+            recv_sem=recv_at,
+            device_id=device,
+            device_id_type=MESH,
+        )
+        copy.start()
+        sent.append(copy)
+        return copy
+
+    own_copies = []
+    for index, weight in enumerate((second_weight, third_weight)):
+        copy = pltpu.make_async_copy(weight, slots.at[index, me], own_sem.at[index])
+        copy.start()
+        own_copies.append(copy)
 
     barrier = pltpu.get_barrier_semaphore()
     for step in range(1, n):
         pl.semaphore_signal(
             barrier, inc=1, device_id={"chan": lax.rem(me + step, n)}, device_id_type=MESH
         )
+    for step in range(1, shards):
+        pl.semaphore_signal(
+            barrier, inc=1, device_id={"tm": lax.rem(shard + step, shards)}, device_id_type=MESH
+        )
+    pl.semaphore_wait(barrier, n + shards - 2)
+
+    following = send(
+        waveform.at[pl.ds(0, after), :],
+        samples.at[pl.ds(HALF + frames, after), :],
+        halo_send.at[0],
+        halo_recv.at[0],
+        tm=lax.rem(shard + shards - 1, shards),
+    )
+    leading = send(
+        waveform.at[pl.ds(frames - HALF, HALF), :],
+        samples.at[pl.ds(0, HALF), :],
+        halo_send.at[1],
+        halo_recv.at[1],
+        tm=lax.rem(shard + 1, shards),
+    )
+    small_copies = [
+        send(
+            small,
+            smalls.at[me],
+            small_send.at[step],
+            small_recv.at[step],
+            chan=lax.rem(me + step, n),
+        )
+        for step in range(1, n)
+    ]
+    weight_chip, weight_pair = [], []
+    for index, weight in enumerate((second_weight, third_weight)):
+        weight_chip.append(
+            [
+                send(
+                    weight,
+                    slots.at[index, me],
+                    weight_send.at[index, step],
+                    weight_recv.at[index, step],
+                    chan=lax.rem(chip + step, chips) * 2 + core,
+                )
+                for step in range(1, chips)
+            ]
+        )
+        weight_pair.append(
+            [
+                send(
+                    weight,
+                    slots.at[index, me],
+                    weight_pair_send.at[index, 0],
+                    weight_pair_recv.at[index, 0],
+                    chan=pair,
+                )
+            ]
+        )
+
+    def forward_weight(index):
+        for step in range(1, chips):
+            other = lax.rem(chip + chips - step, chips) * 2 + core
+            weight_chip[index][step - 1].wait_recv()
+            weight_pair[index].append(
+                send(
+                    slots.at[index, other],
+                    slots.at[index, other],
+                    weight_pair_send.at[index, step],
+                    weight_pair_recv.at[index, step],
+                    chan=pair,
+                )
+            )
+
+    def assemble_weight(index):
+        own_copies[index].wait()
+        for copy in weight_pair[index]:
+            copy.wait_recv()
+        for source in range(n):
+            full[index, :, source * part : (source + 1) * part] = slots[index, source]
 
     tap_copies = []
     for g in range(groups):
@@ -83,7 +207,115 @@
             copy.start()
             tap_copies.append(copy)
 
-    pl.semaphore_wait(barrier, n - 1)
+    samples[HALF : HALF + frames, :] = waveform[...]
+    smalls[me] = small[...]
+    following.wait_recv()
+    leading.wait_recv()
+    for copy in small_copies:
+        copy.wait_recv()
+
+    extra = rows + 16
+    place = me * rows - HALF + lax.broadcasted_iota(jnp.int32, (rows + 32, 1), 0)
+    inside = (shard * frames + place >= 0) & (shard * frames + place < shards * frames)
+    row = lax.broadcasted_iota(jnp.int32, (extra, 1), 0)
+    counted = (place[:extra] >= 0) & (place[:extra] < frames) & (row < rows)
+    held = samples[pl.ds(pl.multiple_of(me * rows, 16), rows + 32), :].astype(jnp.float32)
+    sample32[...] = jnp.where(inside, held, 0.0)
+    patches = (
+        sample32[0:extra, :] + pltpu.roll(sample32[1 : extra + 1, :], 20, axis=1)
+    ).astype(jnp.bfloat16)
+
+    band32[...] = jnp.zeros_like(band32)
+    for f in range(4):
+        for source in range(n):
+            at = f * channels + source * part
+            band32[5 * f : 5 * f + 10, at : at + part] = smalls[source, 0:10, :]
+    moments = jnp.zeros((2, channels), jnp.float32)
+    for f in range(4):
+        lanes = slice(f * channels, (f + 1) * channels)
+        values = jnp.dot(
+            patches, band32[:, lanes].astype(jnp.bfloat16), preferred_element_type=jnp.float32
+        )
+        conv[:, lanes] = values
+        kept = jnp.where(counted, values, 0.0)
+        moments = moments + jnp.concatenate(
+            [jnp.sum(kept, axis=0, keepdims=True), jnp.sum(kept * kept, axis=0, keepdims=True)],
+            axis=0,
+        )
+    own_stats[...] = moments
+    chan_stats[me] = moments
+    moment_copies = [
+        send(
+            own_stats,
+            chan_stats.at[me],
+            moment_send.at[step],
+            moment_recv.at[step],
+            chan=lax.rem(me + step, n),
+        )
+        for step in range(1, n)
+    ]
+    gain = jnp.concatenate([smalls[source, 10:11, :] for source in range(n)], axis=1)
+    offset = jnp.concatenate([smalls[source, 11:12, :] for source in range(n)], axis=1)
+    for copy in moment_copies:
+        copy.wait_recv()
+    moments = chan_stats[0]
+    for index in range(1, n):
+        moments = moments + chan_stats[index]
+    tm_stats[shard] = moments
+    total_copies = [
+        send(
+            tm_stats.at[shard],
+            tm_stats.at[shard],
+            total_send.at[step],
+            total_recv.at[step],
+            tm=lax.rem(shard + step, shards),
+        )
+        for step in range(1, shards)
+    ]
+    x32[n * rows :, :] = jnp.zeros_like(x32[n * rows :, :])
+    x2[...] = jnp.zeros_like(x2)
+    for copy in total_copies:
+        copy.wait_recv()
+    moments = tm_stats[0]
+    for index in range(1, shards):
+        moments = moments + tm_stats[index]
+    moments = moments / (4 * frames * shards)
+    mean = moments[0:1]
+    scale = lax.rsqrt(moments[1:2] - mean * mean + 1e-05)
+
+    for f in range(4):
+        lanes = slice(f * channels, (f + 1) * channels)
+        values = gelu_exact((conv[:, lanes] - mean) * scale * gain + offset)
+        values = jnp.where(inside[:extra], values, 0.0).astype(jnp.bfloat16)
+        first[:, lanes] = values
+        if f == 0:
+            shift32[...] = values.astype(jnp.float32)
+
+    def dot(a, b):
+        return jnp.dot(a, b, preferred_element_type=jnp.float32)
+
+    c = channels
+    forward_weight(0)
+    assemble_weight(0)
+    second[0:rows, :] = gelu_exact(
+        dot(first[0:rows, 2 * c :], full[0, 0 : 2 * c, :])
+        + dot(shift32[1 : rows + 1, :].astype(jnp.bfloat16), full[0, 2 * c :, :])
+    ).astype(jnp.bfloat16)
+    even = gelu_exact(dot(first[:, 0 : 3 * c], full[0])).astype(jnp.bfloat16)
+    shift32[...] = even.astype(jnp.float32)
+    forward_weight(1)
+    assemble_weight(1)
+    third = gelu_exact(
+        dot(even[0:rows], full[1, 0:c, :])
+        + dot(second[0:rows, :], full[1, c : 2 * c, :])
+        + dot(shift32[1 : rows + 1, :].astype(jnp.bfloat16), full[1, 2 * c :, :])
+    )
+    third = third.astype(jnp.bfloat16).astype(jnp.float32)
+    centred = third - jnp.mean(third, axis=1, keepdims=True)
+    spread = jnp.mean(centred * centred, axis=1, keepdims=True)
+    normed[...] = (
+        centred * lax.rsqrt(spread + 1e-05) * feature[0:1, :] + feature[1:2, :]
+    ).astype(jnp.bfloat16)
 
     def block(index):
         return gathered.at[pl.ds(pl.multiple_of(index * rows, 16), rows), :]
@@ -122,8 +354,6 @@
         inside = (frame >= 0) & (frame < shards * frames)
         x32[pl.ds(pl.multiple_of(index * rows, 8), rows), :] = jnp.where(inside, values, 0.0)
 
-    x32[n * rows :, :] = jnp.zeros_like(x32[n * rows :, :])
-    x2[...] = jnp.zeros_like(x2)
     project(me, normed)
     first_pair.wait_recv()
     project(pair, block(pair))
@@ -210,7 +440,7 @@
     gain_bias = params[...].T
     for copy in stat_copies:
         copy.wait_recv()
-    gain, bias = gain_bias[:, 2:3], gain_bias[:, 3:4]
+    last_gain, last_bias = gain_bias[:, 2:3], gain_bias[:, 3:4]
 
     @pl.loop(0, frames // tile)
     def _(m):
@@ -221,35 +451,81 @@
         mean = both[0:1] / model_width
         scale = lax.rsqrt(both[1:2] / model_width - mean * mean + 1e-05)
         out[:, pl.ds(start, tile)] = (
-            (summed[:, pl.ds(start, tile)] - mean) * scale * gain + bias
+            (summed[:, pl.ds(start, tile)] - mean) * scale * last_gain + last_bias
         ).astype(jnp.bfloat16)
 
-    for copy in chip_copies + [first_pair] + forwards + stat_copies:
+    for copy in sent + chip_copies + [first_pair] + forwards + stat_copies:
         copy.wait_send()
 
 
-def tail(normed, project_weight, params, position_weight, n, frames, model_width):
-    rows, channels = normed.shape
+def encoder(
+    waveform,
+    small,
+    second_weight,
+    third_weight,
+    feature,
+    project_weight,
+    params,
+    position_weight,
+    n,
+    shards,
+    model_width,
+):
+    frames = waveform.shape[0]
+    rows = rows_per_device(frames, n)
+    after = -(-(n * rows - HALF - frames + 32) // 16) * 16
+    channels = feature.shape[1]
+    part = channels // n
     width = project_weight.shape[1]
     groups = width // GW
     length = frames + K
     vmem = pl.BlockSpec(memory_space=pltpu.VMEM)
+    anywhere = pl.BlockSpec(memory_space=pl.ANY)
     dma = pltpu.SemaphoreType.DMA
+    half = jnp.bfloat16
+    single = jnp.float32
     return pl.pallas_call(
-        functools.partial(tail_kernel, n, frames, rows, model_width),
-        out_shape=jax.ShapeDtypeStruct((width, frames), jnp.bfloat16),
-        in_specs=[vmem, vmem, vmem, pl.BlockSpec(memory_space=pl.ANY)],
+        functools.partial(encoder_kernel, n, shards, frames, rows, model_width),
+        out_shape=jax.ShapeDtypeStruct((width, frames), half),
+        in_specs=[vmem, vmem, anywhere, anywhere, vmem, vmem, vmem, anywhere],
         out_specs=vmem,
         scratch_shapes=[
-            pltpu.VMEM((n * rows, channels), jnp.bfloat16),
-            pltpu.VMEM((groups, PHASES * GW, SPAN * GW), jnp.bfloat16),
-            pltpu.VMEM((n * rows + 64, width), jnp.float32),
-            pltpu.VMEM((length + 64, 2 * GW), jnp.float32),
-            pltpu.VMEM((length + 16, SPAN // 2 * GW), jnp.bfloat16),
-            pltpu.VMEM((length, PHASES * GW), jnp.float32),
-            pltpu.VMEM((frames, width), jnp.float32),
-            pltpu.VMEM((width, frames), jnp.float32),
-            pltpu.VMEM((n, 2, frames), jnp.float32),
+            pltpu.VMEM((HALF + frames + after, 128), half),
+            pltpu.VMEM((rows + 32, 128), single),
+            pltpu.VMEM((n, 16, part), single),
+            pltpu.VMEM((128, 4 * channels), single),
+            pltpu.VMEM((rows + 16, 4 * channels), single),
+            pltpu.VMEM((rows + 16, 4 * channels), half),
+            pltpu.VMEM((rows + 16, channels), single),
+            pltpu.VMEM((rows, channels), half),
+            pltpu.VMEM((2, n, 3 * channels, part), half),
+            pltpu.VMEM((2, 3 * channels, channels), half),
+            pltpu.VMEM((2, channels), single),
+            pltpu.VMEM((n, 2, channels), single),
+            pltpu.VMEM((shards, 2, channels), single),
+            pltpu.VMEM((rows, channels), half),
+            pltpu.VMEM((n * rows, channels), half),
+            pltpu.VMEM((groups, PHASES * GW, SPAN * GW), half),
+            pltpu.VMEM((n * rows + 64, width), single),
+            pltpu.VMEM((length + 64, 2 * GW), single),
+            pltpu.VMEM((length + 16, SPAN // 2 * GW), half),
+            pltpu.VMEM((length, PHASES * GW), single),
+            pltpu.VMEM((frames, width), single),
+            pltpu.VMEM((width, frames), single),
+            pltpu.VMEM((n, 2, frames), single),
+            dma((2,)),
+            dma((2,)),
+            dma((2,)),
+            dma((n,)),
+            dma((n,)),
+            dma((2, n // 2)),
+            dma((2, n // 2)),
+            dma((2, n // 2)),
+            dma((2, n // 2)),
+            dma((n,)),
+            dma((n,)),
+            dma((shards,)),
+            dma((shards,)),
             dma((groups, PHASES)),
             dma((n // 2,)),
             dma((n // 2,)),
@@ -259,18 +535,19 @@
             dma((n,)),
         ],
         compiler_params=pltpu.CompilerParams(
-            collective_id=0, has_side_effects=True, vmem_limit_bytes=48 * 1024 * 1024
+            collective_id=0, has_side_effects=True, vmem_limit_bytes=56 * 1024 * 1024
         ),
-        name="tail",
-    )(normed, project_weight, params, position_weight)
-
-
-def feature_norm(rows, gain, bias):
-    values = rows.astype(jnp.float32)
-    mean = jnp.mean(values, axis=1, keepdims=True)
-    centred = values - mean
-    spread = jnp.mean(centred * centred, axis=1, keepdims=True)
-    return (centred * lax.rsqrt(spread + 1e-05) * gain + bias).astype(jnp.bfloat16)
+        name="encoder",
+    )(
+        waveform,
+        small,
+        second_weight,
+        third_weight,
+        feature,
+        project_weight,
+        params,
+        position_weight,
+    )
 
 
 def local(
@@ -292,75 +569,35 @@
     n = lax.axis_size("chan")
     me = lax.axis_index("chan")
     shards = lax.axis_size("tm")
-    shard = lax.axis_index("tm")
-    frames = waveform.shape[0] // 20
-    rows = rows_per_device(frames, n)
-    channels = feature_gain.shape[0]
+    channels, part = second_weight.shape[1:]
     width = project_weight.shape[1]
-    model_width = width * n
-
-    weights = lax.all_gather(
-        jnp.concatenate([second_weight, third_weight], 0), "chan", axis=2, tiled=True
-    )
-    second_full = weights[:3].reshape(3 * channels, channels)
-    third_full = weights[3:].reshape(3 * channels, channels)
-    small = lax.all_gather(
-        jnp.concatenate(
-            [first_weight.astype(jnp.float32), instance_gain[None], instance_bias[None]], 0
-        ),
-        "chan",
-        axis=1,
-        tiled=True,
-    )
-    first_full = small[:10].astype(jnp.bfloat16)
-    gain, offset = small[10], small[11]
-
-    after = 20 * (n * rows - HALF - frames) + 40
-    before = 20 * HALF
-    samples = jnp.concatenate(
-        [shifted(waveform[-before:], "tm", 1), waveform, shifted(waveform[:after], "tm", -1)]
-    )
-    mine = lax.dynamic_slice_in_dim(samples, me * rows * 20, (rows + 2) * 20)
-    mine = mine.reshape(rows + 2, 20)
-    patches = jnp.concatenate([mine[:-1], mine[1:, :5]], axis=1)
-    band = jnp.concatenate(
-        [jnp.pad(first_full, ((5 * f, 15 - 5 * f), (0, 0))) for f in range(4)], axis=1
-    )
-    conv = jnp.dot(patches, band, preferred_element_type=jnp.float32)
-    place = me * rows - HALF + jnp.arange(rows + 1)[:, None]
-    counted = (place >= 0) & (place < frames) & (jnp.arange(rows + 1)[:, None] < rows)
-    kept = jnp.where(counted, conv, 0.0)
-    sums = jnp.stack([jnp.sum(kept, axis=0), jnp.sum(kept * kept, axis=0)])
-    sums = jnp.sum(sums.reshape(2, 4, channels), axis=1)
-    sums = lax.psum(sums, ("tm", "chan"))
-    count = 4 * frames * shards
-    mean_first = sums[0] / count
-    var_first = sums[1] / count - mean_first * mean_first
-    scale = lax.rsqrt(var_first + 1e-05)
-    spread = [jnp.tile(v, 4) for v in (mean_first, scale, gain, offset)]
-    first = gelu_exact((conv - spread[0]) * spread[1] * spread[2] + spread[3])
-    inside = (shard * frames + place >= 0) & (shard * frames + place < shards * frames)
-    first = jnp.where(inside, first, 0.0).astype(jnp.bfloat16)
-
-    def dot(a, b):
-        return jnp.dot(a, b, preferred_element_type=jnp.float32)
-
-    c = channels
-    second_even = gelu_exact(dot(first[:, : 3 * c], second_full)).astype(jnp.bfloat16)
-    second_odd = gelu_exact(
-        dot(first[:-1, 2 * c :], second_full[: 2 * c]) + dot(first[1:, :c], second_full[2 * c :])
-    ).astype(jnp.bfloat16)
-    third = gelu_exact(
-        dot(second_even[:-1], third_full[:c])
-        + dot(second_odd, third_full[c : 2 * c])
-        + dot(second_even[1:], third_full[2 * c :])
-    ).astype(jnp.bfloat16)
-    normed = feature_norm(third, feature_gain, feature_bias)
-
+    blocks = jnp.pad(waveform.reshape(-1, 20), ((0, 0), (0, 108)))
+    small = jnp.concatenate(
+        [
+            first_weight.astype(jnp.float32),
+            instance_gain[None],
+            instance_bias[None],
+            jnp.zeros((4, part), jnp.float32),
+        ],
+        0,
+    )
     bias_here = lax.dynamic_slice_in_dim(project_bias, me * width, width)
     params = jnp.stack([bias_here, position_bias, final_gain, final_bias])
     params = jnp.pad(params, ((0, 4), (0, 0)))
-    return tail(normed, project_weight, params, position_weight, n, frames, model_width)
+    feature = jnp.stack([feature_gain, feature_bias])
+    return encoder(
+        blocks,
+        small,
+        second_weight.reshape(3 * channels, part),
+        third_weight.reshape(3 * channels, part),
+        feature,
+        project_weight,
+        params,
+        position_weight,
+        n,
+        shards,
+        width * n,
+    )
 
 
 def solution(mesh):

time: 118 us -> 76 us (0.64)
  blocking collectives: 40.4 us -> 0 us
  Pallas kernels: 30.7 us -> 65.8 us
  between operations: 13.7 us -> 0.02 us
  matrix products: 10.5 us -> 0 us
  starting transfers between devices: 6.2 us -> 0 us
  local copies, waits for them, and re-layouts: 8.45 us -> 5.19 us
  other arithmetic: 7.69 us -> 4.61 us
    psum x1 -> x0, blocking collectives: 35.2 us -> none  [local(): sums = lax.psum(sums, ('tm', 'chan'))]
    pallas_call x1, Pallas kernels: 30.7 us -> 65.8 us  [encoder(): pl.pallas_call(functools.partial(encoder_kernel, n, shards, frames, rows,...]
    dot_general x6 -> x0, matrix products: 10.5 us -> none  [the longest x5 9.82 us: dot(): return jnp.dot(a, b, preferred_element_type=jnp.float32)]
    ppermute x2 -> x0, starting transfers between devices: 6.2 us -> none  [shifted(): lax.ppermute(value, axis, [(source, source + steps) for source in range(l...]
    all_gather x1 -> x0, blocking collectives: 5.18 us -> none  [local(): lax.all_gather(jnp.concatenate([first_weight.astype(jnp.float32), instanc...]
    slice x11 -> x0, local copies, waits for them, and re-layouts: 3.16 us -> none  [the longest x1 1.29 us: local(): second_full[:2 * c]]
    concatenate x2 -> x0, other arithmetic: 2.93 us -> none  [the longest x1 2.07 us: local(): jnp.concatenate([second_weight, third_weight], 0)]
    convert_element_type x2 -> x0, other arithmetic: 2.32 us -> none  [the longest x1 2.12 us: local(): first = jnp.where(inside, first, 0.0).astype(jnp.bfloat16)]
  transfers between devices with their start and end apart: 3 -> 0, of which waited for: 0 -> 0; matrix products, arithmetic and copies ran while one was open for 7% -> 0% of each run, Pallas kernels for 0% -> 0%
where the time goes in v1:
time: 76 us; the launch traced here: 75.6 us
  Pallas kernels  65.8 us (87%)
  local copies, waits for them, and re-layouts  5.19 us (7%)
  other arithmetic  4.61 us (6%)
    pallas_call x1, Pallas kernels, encoder(): pl.pallas_call(functools.partial(encoder_kernel, n, shards, frames, rows,...  65.8 us
    unnamed x1, local copies, waits for them, and re-layouts  1.97 us
    reshape x1, local copies, waits for them, and re-layouts, local(): blocks = jnp.pad(waveform.reshape(-1, 20), ((0, 0), (0, 108)))  1.6 us

profile of v1, /device:TPU:0, one launch (start us, length us, event | category | flops | bytes accessed | tf_op | source)
XLA Modules:
  0.0 75.6 jit_solution(10579863643308570382)
XLA Ops:
  0.0 0.8 %dynamic_slice.3 = f32[256]{0:T(256)S(1)} dynamic-slice(f32[1024]{0:T(1024)} %param.23, s32[]{:T(128)S(6)} %select_n.3), dynamic_slice_sizes={256} | dynamic-slice | bytes 2052 | tf_op jit(solution)/shard_map/dynamic_slice | solution.py:584
  0.8 0.1 pad.19.clone
  0.8 1.3 %pad_maximum_fusion.feature = f32[2,512]{1,0:T(2,128)} fusion(f32[1,512]{1,0:T(1,128)} %bitcast.13, f32[1,512]{1,0:T(1,128)} %bitcast.14), kind=kLoop, calls=%fused_computation.5 | loop fusion | flops 1024 | bytes 8192 | tf_op jit(solution)/shard_map/stack | solution.py:587
  2.1 1.3 %select_maximum_fusion.params = f32[8,256]{1,0:T(8,128)} fusion(f32[1,256]{1,0:T(1,128)} %bitcast.15, f32[1,256]{1,0:T(1,128)} %bitcast.16, f32[1,256]{1,0:T(1,128)} %bitcast.17, f32[1,256]{1,0:T(1,128)S(1)} %bitcast.12), kind=kLoop, calls=%fused_computation | loop fusion | flops 16384 | bytes 12288 | tf_op jit(solution)/shard_map/stack | solution.py:585
  3.4 0.7 convert_element_type.7
  4.1 1.3 %maximum_maximum_fusion.small = f32[16,128]{1,0:T(8,128)} fusion(f32[1,128]{1,0:T(1,128)} %bitcast.18, f32[1,128]{1,0:T(1,128)} %bitcast.19, f32[10,128]{1,0:T(8,128)S(1)} %convert_element_type.7, f32[16]{0:T(128)S(1)} %pad.19.clone), kind=kLoop, calls=%fused_computation.4 | loop fusion | flops 6144 | bytes 14400 | tf_op jit(solution)/shard_map/concatenate | solution.py:575
  5.5 1.6 %reshape.9 = bf16[1280,20]{1,0:T(8,128)(2,1)S(1)} reshape(bf16[25600]{0:T(1024)(128)(2,1)} %param.14) | data formatting | bytes 102400 | tf_op jit(solution)/shard_map/reshape | solution.py:574
  7.1 0.8 %pad.8.waveform = bf16[1280,128]{1,0:T(8,128)(2,1)} pad(bf16[1280,20]{1,0:T(8,128)(2,1)S(1)} %reshape.9, bf16[]{:T(256)} %constant.3.clone.1), padding=0_0x0_108 | pad | bytes 378882 | tf_op jit(solution)/shard_map/jit(_pad)/pad | solution.py:574
  7.8 65.8 %encoder.1 = bf16[256,1280]{1,0:T(8,128)(2,1)} custom-call(bf16[1280,128]{1,0:T(8,128)(2,1)} %pad.8.waveform, f32[16,128]{1,0:T(8,128)} %maximum_maximum_fusion.small, bf16[1536,128]{1,0:T(8,128)(2,1)} %bitcast.10, bf16[1536,128]{1,0:T(8,128)(2,1)} %bitcast.11, f32[2,512]{1,0:T(2,128)} %pad_maximum_fusion.feature, bf16[512,256]{1,0:T(8,128)(2,1)} %project_weight.1, ...), custom_call_target="tpu_custom_call" | custom-call | tf_op jit(solution)/shard_map/encoder/pallas_call | solution.py:487
  73.7 2.0 %copy.16 = bf16[256,1280]{1,0:T(8,128)(2,1)} copy(bf16[256,1280]{1,0:T(8,128)(2,1)} %encoder.1) | data formatting | bytes 1310720
  (1 shorter events, 0.0 us)

commit v2 on v1

--- a/solution.py
+++ b/solution.py
@@ -30,15 +30,22 @@
     frames,
     rows,
     model_width,
-    waveform,
-    small,
+    wave,
+    first_weight,
+    instance_gain,
+    instance_bias,
     second_weight,
     third_weight,
-    feature,
+    feature_gain,
+    feature_bias,
     project_weight,
+    project_bias,
+    position_weight,
+    position_bias,
+    summed,
+    norm,
+    waveform,
     params,
-    position_weight,
-    out,
     samples,
     sample32,
     smalls,
@@ -60,7 +67,6 @@
     window,
     partial,
     positional,
-    summed,
     stats,
     own_sem,
     halo_send,
@@ -71,6 +77,8 @@
     weight_recv,
     weight_pair_send,
     weight_pair_recv,
+    rec_send,
+    rec_recv,
     moment_send,
     moment_recv,
     total_send,
@@ -85,12 +93,14 @@
 ):
     me = lax.axis_index("chan")
     shard = lax.axis_index("tm")
+    rec = lax.axis_index("rec")
+    recs = lax.axis_size("rec")
     chips = n // 2
     chip, core = me // 2, lax.rem(me, 2)
     pair = chip * 2 + 1 - core
-    width = out.shape[0]
+    width = summed.shape[0]
     groups = width // GW
-    channels = feature.shape[1]
+    channels = feature_gain.shape[1]
     part = channels // n
     after = samples.shape[0] - HALF - frames
     sent = []
@@ -123,7 +133,22 @@
         pl.semaphore_signal(
             barrier, inc=1, device_id={"tm": lax.rem(shard + step, shards)}, device_id_type=MESH
         )
-    pl.semaphore_wait(barrier, n + shards - 2)
+    for step in range(1, recs):
+        pl.semaphore_signal(
+            barrier, inc=1, device_id={"rec": lax.rem(rec + step, recs)}, device_id_type=MESH
+        )
+    waveform[...] = jnp.zeros_like(waveform)
+    waveform[:, 0:20] = wave[...]
+    smalls[me] = jnp.concatenate(
+        [
+            first_weight[...].astype(jnp.float32),
+            instance_gain[...],
+            instance_bias[...],
+            jnp.zeros((4, part), jnp.float32),
+        ],
+        axis=0,
+    )
+    pl.semaphore_wait(barrier, n + shards + recs - 3)
 
     following = send(
         waveform.at[pl.ds(0, after), :],
@@ -141,7 +166,7 @@
     )
     small_copies = [
         send(
-            small,
+            smalls.at[me],
             smalls.at[me],
             small_send.at[step],
             small_recv.at[step],
@@ -149,13 +174,18 @@
         )
         for step in range(1, n)
     ]
-    weight_chip, weight_pair = [], []
+    weight_chip, weight_pair, weight_rec = [], [], [[], []]
+    depth = 3 * channels // recs
+
+    def share(owner):
+        return pl.ds(pl.multiple_of(owner * depth, 16), depth)
+
     for index, weight in enumerate((second_weight, third_weight)):
         weight_chip.append(
             [
                 send(
-                    weight,
-                    slots.at[index, me],
+                    weight.at[share(rec), :],
+                    slots.at[index, me, share(rec), :],
                     weight_send.at[index, step],
                     weight_recv.at[index, step],
                     chan=lax.rem(chip + step, chips) * 2 + core,
@@ -168,26 +198,54 @@
                 send(
                     weight,
                     slots.at[index, me],
-                    weight_pair_send.at[index, 0],
-                    weight_pair_recv.at[index, 0],
+                    weight_pair_send.at[index, 0, 0],
+                    weight_pair_recv.at[index, 0, 0],
                     chan=pair,
                 )
             ]
         )
 
-    def forward_weight(index):
+    def forward_chip(index):
         for step in range(1, chips):
             other = lax.rem(chip + chips - step, chips) * 2 + core
+            piece = slots.at[index, other, share(rec), :]
             weight_chip[index][step - 1].wait_recv()
+            for turn in range(1, recs):
+                weight_rec[index].append(
+                    send(
+                        piece,
+                        piece,
+                        rec_send.at[index, step, turn],
+                        rec_recv.at[index, step, turn],
+                        rec=lax.rem(rec + turn, recs),
+                    )
+                )
             weight_pair[index].append(
                 send(
-                    slots.at[index, other],
-                    slots.at[index, other],
-                    weight_pair_send.at[index, step],
-                    weight_pair_recv.at[index, step],
+                    piece,
+                    piece,
+                    weight_pair_send.at[index, step, 0],
+                    weight_pair_recv.at[index, step, 0],
                     chan=pair,
                 )
             )
+
+    def forward_rec(index):
+        arrivals = iter(weight_rec[index])
+        for step in range(1, chips):
+            other = lax.rem(chip + chips - step, chips) * 2 + core
+            for turn in range(1, recs):
+                piece = slots.at[index, other, share(lax.rem(rec + recs - turn, recs)), :]
+                next(arrivals).wait_recv()
+                weight_pair[index].append(
+                    send(
+                        piece,
+                        piece,
+                        weight_pair_send.at[index, step, turn],
+                        weight_pair_recv.at[index, step, turn],
+                        chan=pair,
+                    )
+                )
 
     def assemble_weight(index):
         own_copies[index].wait()
@@ -208,7 +266,12 @@
             tap_copies.append(copy)
 
     samples[HALF : HALF + frames, :] = waveform[...]
-    smalls[me] = small[...]
+    chosen = project_bias[:, 0:width]
+    for source in range(1, n):
+        chosen = jnp.where(me == source, project_bias[:, source * width : (source + 1) * width], chosen)
+    params[...] = jnp.concatenate(
+        [chosen, position_bias[...], jnp.zeros((6, width), jnp.float32)], axis=0
+    )
     following.wait_recv()
     leading.wait_recv()
     for copy in small_copies:
@@ -256,6 +319,7 @@
     ]
     gain = jnp.concatenate([smalls[source, 10:11, :] for source in range(n)], axis=1)
     offset = jnp.concatenate([smalls[source, 11:12, :] for source in range(n)], axis=1)
+    forward_chip(0)
     for copy in moment_copies:
         copy.wait_recv()
     moments = chan_stats[0]
@@ -283,6 +347,8 @@
     mean = moments[0:1]
     scale = lax.rsqrt(moments[1:2] - mean * mean + 1e-05)
 
+    forward_chip(1)
+    forward_rec(0)
     for f in range(4):
         lanes = slice(f * channels, (f + 1) * channels)
         values = gelu_exact((conv[:, lanes] - mean) * scale * gain + offset)
@@ -295,7 +361,7 @@
         return jnp.dot(a, b, preferred_element_type=jnp.float32)
 
     c = channels
-    forward_weight(0)
+    forward_rec(1)
     assemble_weight(0)
     second[0:rows, :] = gelu_exact(
         dot(first[0:rows, 2 * c :], full[0, 0 : 2 * c, :])
@@ -303,7 +369,6 @@
     ).astype(jnp.bfloat16)
     even = gelu_exact(dot(first[:, 0 : 3 * c], full[0])).astype(jnp.bfloat16)
     shift32[...] = even.astype(jnp.float32)
-    forward_weight(1)
     assemble_weight(1)
     third = gelu_exact(
         dot(even[0:rows], full[1, 0:c, :])
@@ -314,7 +379,7 @@
     centred = third - jnp.mean(third, axis=1, keepdims=True)
     spread = jnp.mean(centred * centred, axis=1, keepdims=True)
     normed[...] = (
-        centred * lax.rsqrt(spread + 1e-05) * feature[0:1, :] + feature[1:2, :]
+        centred * lax.rsqrt(spread + 1e-05) * feature_gain[...] + feature_bias[...]
     ).astype(jnp.bfloat16)
 
     def block(index):
@@ -437,22 +502,14 @@
         )
         copy.start()
         stat_copies.append(copy)
-    gain_bias = params[...].T
     for copy in stat_copies:
         copy.wait_recv()
-    last_gain, last_bias = gain_bias[:, 2:3], gain_bias[:, 3:4]
-
-    @pl.loop(0, frames // tile)
-    def _(m):
-        start = pl.multiple_of(m * tile, tile)
-        both = stats[0, 0:2, pl.ds(start, tile)]
-        for index in range(1, n):
-            both = both + stats[index, 0:2, pl.ds(start, tile)]
-        mean = both[0:1] / model_width
-        scale = lax.rsqrt(both[1:2] / model_width - mean * mean + 1e-05)
-        out[:, pl.ds(start, tile)] = (
-            (summed[:, pl.ds(start, tile)] - mean) * scale * last_gain + last_bias
-        ).astype(jnp.bfloat16)
+    both = stats[0]
+    for index in range(1, n):
+        both = both + stats[index]
+    mean = both[0:1] / model_width
+    norm[0:1, :] = mean
+    norm[1:2, :] = lax.rsqrt(both[1:2] / model_width - mean * mean + 1e-05)
 
     for copy in sent + chip_copies + [first_pair] + forwards + stat_copies:
         copy.wait_send()
@@ -460,13 +517,17 @@
 
 def encoder(
     waveform,
-    small,
+    first_weight,
+    instance_gain,
+    instance_bias,
     second_weight,
     third_weight,
-    feature,
+    feature_gain,
+    feature_bias,
     project_weight,
-    params,
+    project_bias,
     position_weight,
+    position_bias,
     n,
     shards,
     model_width,
@@ -474,8 +535,9 @@
     frames = waveform.shape[0]
     rows = rows_per_device(frames, n)
     after = -(-(n * rows - HALF - frames + 32) // 16) * 16
-    channels = feature.shape[1]
+    channels = feature_gain.shape[1]
     part = channels // n
+    recs = lax.axis_size("rec")
     width = project_weight.shape[1]
     groups = width // GW
     length = frames + K
@@ -486,10 +548,15 @@
     single = jnp.float32
     return pl.pallas_call(
         functools.partial(encoder_kernel, n, shards, frames, rows, model_width),
-        out_shape=jax.ShapeDtypeStruct((width, frames), half),
-        in_specs=[vmem, vmem, anywhere, anywhere, vmem, vmem, vmem, anywhere],
-        out_specs=vmem,
+        out_shape=[
+            jax.ShapeDtypeStruct((width, frames), single),
+            jax.ShapeDtypeStruct((2, frames), single),
+        ],
+        in_specs=[vmem] * 4 + [anywhere] * 2 + [vmem] * 4 + [anywhere, vmem],
+        out_specs=[vmem, vmem],
         scratch_shapes=[
+            pltpu.VMEM((frames, 128), half),
+            pltpu.VMEM((8, width), single),
             pltpu.VMEM((HALF + frames + after, 128), half),
             pltpu.VMEM((rows + 32, 128), single),
             pltpu.VMEM((n, 16, part), single),
@@ -511,7 +578,6 @@
             pltpu.VMEM((length + 16, SPAN // 2 * GW), half),
             pltpu.VMEM((length, PHASES * GW), single),
             pltpu.VMEM((frames, width), single),
-            pltpu.VMEM((width, frames), single),
             pltpu.VMEM((n, 2, frames), single),
             dma((2,)),
             dma((2,)),
@@ -520,8 +586,10 @@
             dma((n,)),
             dma((2, n // 2)),
             dma((2, n // 2)),
-            dma((2, n // 2)),
-            dma((2, n // 2)),
+            dma((2, n // 2, recs)),
+            dma((2, n // 2, recs)),
+            dma((2, n // 2, recs)),
+            dma((2, n // 2, recs)),
             dma((n,)),
             dma((n,)),
             dma((shards,)),
@@ -540,13 +608,17 @@
         name="encoder",
     )(
         waveform,
-        small,
+        first_weight,
+        instance_gain,
+        instance_bias,
         second_weight,
         third_weight,
-        feature,
+        feature_gain,
+        feature_bias,
         project_weight,
-        params,
+        project_bias,
         position_weight,
+        position_bias,
     )
 
 
@@ -567,37 +639,28 @@
     final_bias,
 ):
     n = lax.axis_size("chan")
-    me = lax.axis_index("chan")
     shards = lax.axis_size("tm")
     channels, part = second_weight.shape[1:]
     width = project_weight.shape[1]
-    blocks = jnp.pad(waveform.reshape(-1, 20), ((0, 0), (0, 108)))
-    small = jnp.concatenate(
-        [
-            first_weight.astype(jnp.float32),
-            instance_gain[None],
-            instance_bias[None],
-            jnp.zeros((4, part), jnp.float32),
-        ],
-        0,
-    )
-    bias_here = lax.dynamic_slice_in_dim(project_bias, me * width, width)
-    params = jnp.stack([bias_here, position_bias, final_gain, final_bias])
-    params = jnp.pad(params, ((0, 4), (0, 0)))
-    feature = jnp.stack([feature_gain, feature_bias])
-    return encoder(
-        blocks,
-        small,
+    summed, norm = encoder(
+        waveform.reshape(-1, 20),
+        first_weight,
+        instance_gain[None],
+        instance_bias[None],
         second_weight.reshape(3 * channels, part),
         third_weight.reshape(3 * channels, part),
-        feature,
+        feature_gain[None],
+        feature_bias[None],
         project_weight,
-        params,
+        project_bias[None],
         position_weight,
+        position_bias[None],
         n,
         shards,
         width * n,
     )
+    encoded = (summed - norm[0:1]) * norm[1:2] * final_gain[:, None] + final_bias[:, None]
+    return encoded.astype(jnp.bfloat16)
 
 
 def solution(mesh):

time: 76 us -> 64.8 us (0.85)
  Pallas kernels: 65.8 us -> 59 us
  other arithmetic: 4.61 us -> 2.44 us
  local copies, waits for them, and re-layouts: 5.19 us -> 3.14 us
    pallas_call x1, Pallas kernels: 65.8 us -> 59 us  [encoder(): pl.pallas_call(functools.partial(encoder_kernel, n, shards, frames, rows,...]
    another operation x2 -> x0, other arithmetic: 2.6 us -> none  [the longest x1 1.31 us: local(): params = jnp.stack([bias_here, position_bias, final_gain, final_bias])]
    unnamed x1 -> x4, local copies, waits for them, and re-layouts: 1.97 us -> 0.01 us
    convert_element_type x1, other arithmetic: 0.69 us -> 2.44 us  [local(): return encoded.astype(jnp.bfloat16)]
    concatenate x1 -> x0, other arithmetic: 1.32 us -> none  [local(): jnp.concatenate([first_weight.astype(jnp.float32), instance_gain[None], i...]
    slice x0 -> x1, local copies, waits for them, and re-layouts: none -> 0.81 us  [local(): norm[0:1]]
    pad x1 -> x0, local copies, waits for them, and re-layouts: 0.79 us -> none  [local(): blocks = jnp.pad(waveform.reshape(-1, 20), ((0, 0), (0, 108)))]
where the time goes in v2:
time: 64.8 us; the launch traced here: 64.6 us
  Pallas kernels  59 us (91%)
  local copies, waits for them, and re-layouts  3.14 us (5%)
  other arithmetic  2.44 us (4%)
    pallas_call x1, Pallas kernels, encoder(): pl.pallas_call(functools.partial(encoder_kernel, n, shards, frames, rows,...  59 us
    convert_element_type x1, other arithmetic, local(): return encoded.astype(jnp.bfloat16)  2.44 us
    reshape x1, local copies, waits for them, and re-layouts, local(): waveform.reshape(-1, 20)  2.33 us

profile of v2, /device:TPU:0, one launch (start us, length us, event | category | flops | bytes accessed | tf_op | source)
XLA Modules:
  0.0 64.6 jit_solution(3197594658318363310)
XLA Ops:
  0.0 2.3 %reshape.11.wave = bf16[1280,20]{1,0:T(8,128)(2,1)} reshape(bf16[25600]{0:T(1024)(128)(2,1)} %param.14) | data formatting | bytes 102400 | tf_op jit(solution)/shard_map/reshape | solution.py:646
  2.3 0.0 copy-start
  2.3 0.0 copy-start.1
  2.3 59.0 %encoder.1 = (f32[256,1280]{1,0:T(8,128)}, f32[2,1280]{1,0:T(2,128)}) custom-call(bf16[1280,20]{1,0:T(8,128)(2,1)} %reshape.11.wave, bf16[10,128]{1,0:T(8,128)(2,1)} %first_weight.1, f32[1,128]{1,0:T(1,128)} %bitcast.14, f32[1,128]{1,0:T(1,128)} %bitcast.15, bf16[1536,128]{1,0:T(8,128)(2,1)} %bitcast.8, bf16[1536,128]{1,0:T(8,128)(2,1)} %bitcast.9, ...), custom_call_target="tpu_custom_call" | custom-call | tf_op jit(solution)/shard_map/encoder/pallas_call | solution.py:549
  61.3 0.8 %slice_reduce_fusion.1 = (f32[1280]{0:T(1024)S(1)}, f32[1280]{0:T(1024)S(1)}) fusion(f32[2,1280]{1,0:T(2,128)} %get-tuple-element.8), kind=kLoop, calls=%fused_computation.2 | loop fusion | bytes 20480 | tf_op jit(solution)/shard_map/slice | solution.py:662
  62.1 0.0 copy-done
  62.1 0.0 copy-done.1
  62.1 2.4 %add_convert_fusion = bf16[256,1280]{1,0:T(8,128)(2,1)} fusion(f32[256,1280]{1,0:T(8,128)} %get-tuple-element.7, f32[256]{0:T(256)S(1)} %copy-done, f32[256]{0:T(256)S(1)} %copy-done.1, f32[1280]{0:T(1024)S(1)} %get-tuple-element.10, f32[1280]{0:T(1024)S(1)} %get-tuple-element.9), kind=kLoop, calls=%fused_computation | loop fusion | flops 1638400 | bytes 1978368 | tf_op jit(solution)/shard_map/convert_element_type | solution.py:663
Async XLA Ops:
  2.3 59.8 %copy-start = (f32[256]{0:T(256)S(1)}, f32[256]{0:T(256)}, u32[]{:S(2)}) copy-start(f32[256]{0:T(256)} %param.27) | copy-start | bytes 3076
  2.3 59.8 %copy-start.1 = (f32[256]{0:T(256)S(1)}, f32[256]{0:T(256)}, u32[]{:S(2)}) copy-start(f32[256]{0:T(256)} %param.26) | copy-start | bytes 3076

commit v3 on v2

--- a/solution.py
+++ b/solution.py
@@ -370,42 +370,51 @@
     even = gelu_exact(dot(first[:, 0 : 3 * c], full[0])).astype(jnp.bfloat16)
     shift32[...] = even.astype(jnp.float32)
     assemble_weight(1)
-    third = gelu_exact(
-        dot(even[0:rows], full[1, 0:c, :])
-        + dot(second[0:rows, :], full[1, c : 2 * c, :])
-        + dot(shift32[1 : rows + 1, :].astype(jnp.bfloat16), full[1, 2 * c :, :])
-    )
-    third = third.astype(jnp.bfloat16).astype(jnp.float32)
-    centred = third - jnp.mean(third, axis=1, keepdims=True)
-    spread = jnp.mean(centred * centred, axis=1, keepdims=True)
-    normed[...] = (
-        centred * lax.rsqrt(spread + 1e-05) * feature_gain[...] + feature_bias[...]
-    ).astype(jnp.bfloat16)
-
     def block(index):
         return gathered.at[pl.ds(pl.multiple_of(index * rows, 16), rows), :]
 
-    chip_copies = []
-    for step in range(1, chips):
-        copy = pltpu.make_async_remote_copy(
-            src_ref=normed,
-            dst_ref=block(me),
-            send_sem=send_sem.at[step],
-            recv_sem=recv_sem.at[step],
-            device_id={"chan": lax.rem(chip + step, chips) * 2 + core},
-            device_id_type=MESH,
-        )
-        copy.start()
-        chip_copies.append(copy)
-    first_pair = pltpu.make_async_remote_copy(
-        src_ref=normed,
-        dst_ref=block(me),
-        send_sem=pair_send.at[0],
-        recv_sem=pair_recv.at[0],
-        device_id={"chan": pair},
-        device_id_type=MESH,
-    )
-    first_pair.start()
+    pieces = 2 if rows % 32 == 0 else 1
+    size = rows // pieces
+
+    def piece(index, h):
+        return gathered.at[pl.ds(pl.multiple_of(index * rows + h * size, 16), size), :]
+
+    chip_copies, first_pair = [], []
+    for h in range(pieces):
+        own = slice(h * size, (h + 1) * size)
+        third = gelu_exact(
+            dot(even[own], full[1, 0:c, :])
+            + dot(second[own, :], full[1, c : 2 * c, :])
+            + dot(
+                shift32[h * size + 1 : (h + 1) * size + 1, :].astype(jnp.bfloat16),
+                full[1, 2 * c :, :],
+            )
+        )
+        third = third.astype(jnp.bfloat16).astype(jnp.float32)
+        centred = third - jnp.mean(third, axis=1, keepdims=True)
+        spread = jnp.mean(centred * centred, axis=1, keepdims=True)
+        normed[own, :] = (
+            centred * lax.rsqrt(spread + 1e-05) * feature_gain[...] + feature_bias[...]
+        ).astype(jnp.bfloat16)
+        for step in range(1, chips):
+            chip_copies.append(
+                send(
+                    normed.at[pl.ds(h * size, size), :],
+                    piece(me, h),
+                    send_sem.at[step, h],
+                    recv_sem.at[step, h],
+                    chan=lax.rem(chip + step, chips) * 2 + core,
+                )
+            )
+        first_pair.append(
+            send(
+                normed.at[pl.ds(h * size, size), :],
+                piece(me, h),
+                pair_send.at[0, h],
+                pair_recv.at[0, h],
+                chan=pair,
+            )
+        )
 
     def project(index, source):
         values = jnp.dot(source[...], project_weight[...], preferred_element_type=jnp.float32)
@@ -420,26 +429,30 @@
         x32[pl.ds(pl.multiple_of(index * rows, 8), rows), :] = jnp.where(inside, values, 0.0)
 
     project(me, normed)
-    first_pair.wait_recv()
+    for copy in first_pair:
+        copy.wait_recv()
     project(pair, block(pair))
     forwards = []
+    for h in range(pieces):
+        for step in range(1, chips):
+            other = lax.rem(chip + chips - step, chips) * 2 + core
+            chip_copies[h * (chips - 1) + step - 1].wait_recv()
+            forwards.append(
+                send(
+                    piece(other, h),
+                    piece(other, h),
+                    pair_send.at[step, h],
+                    pair_recv.at[step, h],
+                    chan=pair,
+                )
+            )
     for step in range(1, chips):
         other = lax.rem(chip + chips - step, chips) * 2 + core
-        chip_copies[step - 1].wait_recv()
-        copy = pltpu.make_async_remote_copy(
-            src_ref=block(other),
-            dst_ref=block(other),
-            send_sem=pair_send.at[step],
-            recv_sem=pair_recv.at[step],
-            device_id={"chan": pair},
-            device_id_type=MESH,
-        )
-        copy.start()
-        forwards.append(copy)
         project(other, block(other))
+    for copy in forwards:
+        copy.wait_recv()
     for step in range(1, chips):
         other = lax.rem(chip + chips - step, chips) * 2 + 1 - core
-        forwards[step - 1].wait_recv()
         project(other, block(other))
 
     length = frames + K
@@ -511,7 +524,7 @@
     norm[0:1, :] = mean
     norm[1:2, :] = lax.rsqrt(both[1:2] / model_width - mean * mean + 1e-05)
 
-    for copy in sent + chip_copies + [first_pair] + forwards + stat_copies:
+    for copy in sent + stat_copies:
         copy.wait_send()
 
 
@@ -595,10 +608,10 @@
             dma((shards,)),
             dma((shards,)),
             dma((groups, PHASES)),
-            dma((n // 2,)),
-            dma((n // 2,)),
-            dma((n // 2,)),
-            dma((n // 2,)),
+            dma((n // 2, 2)),
+            dma((n // 2, 2)),
+            dma((n // 2, 2)),
+            dma((n // 2, 2)),
             dma((n,)),
             dma((n,)),
         ],

time: 64.8 us -> 64.4 us (level)
  no operation moved by 1% of the time
where the time goes in v3:
time: 64.4 us; the launch traced here: 64.1 us
  Pallas kernels  58.5 us (91%)
  local copies, waits for them, and re-layouts  3.14 us (5%)
  other arithmetic  2.44 us (4%)
    pallas_call x1, Pallas kernels, encoder(): pl.pallas_call(functools.partial(encoder_kernel, n, shards, frames, rows,...  58.5 us
    convert_element_type x1, other arithmetic, local(): return encoded.astype(jnp.bfloat16)  2.44 us
    reshape x1, local copies, waits for them, and re-layouts, local(): waveform.reshape(-1, 20)  2.33 us

profile of v3, /device:TPU:0, one launch (start us, length us, event | category | flops | bytes accessed | tf_op | source)
XLA Modules:
  0.0 64.1 jit_solution(8788985534317263717)
XLA Ops:
  0.0 2.3 %reshape.11.wave = bf16[1280,20]{1,0:T(8,128)(2,1)} reshape(bf16[25600]{0:T(1024)(128)(2,1)} %param.14) | data formatting | bytes 102400 | tf_op jit(solution)/shard_map/reshape | solution.py:659
  2.3 0.0 copy-start
  2.3 0.0 copy-start.1
  2.3 58.5 %encoder.1 = (f32[256,1280]{1,0:T(8,128)}, f32[2,1280]{1,0:T(2,128)}) custom-call(bf16[1280,20]{1,0:T(8,128)(2,1)} %reshape.11.wave, bf16[10,128]{1,0:T(8,128)(2,1)} %first_weight.1, f32[1,128]{1,0:T(1,128)} %bitcast.14, f32[1,128]{1,0:T(1,128)} %bitcast.15, bf16[1536,128]{1,0:T(8,128)(2,1)} %bitcast.8, bf16[1536,128]{1,0:T(8,128)(2,1)} %bitcast.9, ...), custom_call_target="tpu_custom_call" | custom-call | tf_op jit(solution)/shard_map/encoder/pallas_call | solution.py:562
  60.8 0.8 %slice_reduce_fusion.1 = (f32[1280]{0:T(1024)S(1)}, f32[1280]{0:T(1024)S(1)}) fusion(f32[2,1280]{1,0:T(2,128)} %get-tuple-element.8), kind=kLoop, calls=%fused_computation.2 | loop fusion | bytes 20480 | tf_op jit(solution)/shard_map/slice | solution.py:675
  61.6 0.0 copy-done
  61.6 0.0 copy-done.1
  61.6 2.4 %add_convert_fusion = bf16[256,1280]{1,0:T(8,128)(2,1)} fusion(f32[256,1280]{1,0:T(8,128)} %get-tuple-element.7, f32[256]{0:T(256)S(1)} %copy-done, f32[256]{0:T(256)S(1)} %copy-done.1, f32[1280]{0:T(1024)S(1)} %get-tuple-element.10, f32[1280]{0:T(1024)S(1)} %get-tuple-element.9), kind=kLoop, calls=%fused_computation | loop fusion | flops 1638400 | bytes 1978368 | tf_op jit(solution)/shard_map/convert_element_type | solution.py:676
Async XLA Ops:
  2.3 59.3 %copy-start = (f32[256]{0:T(256)S(1)}, f32[256]{0:T(256)}, u32[]{:S(2)}) copy-start(f32[256]{0:T(256)} %param.27) | copy-start | bytes 3076
  2.3 59.3 %copy-start.1 = (f32[256]{0:T(256)S(1)}, f32[256]{0:T(256)}, u32[]{:S(2)}) copy-start(f32[256]{0:T(256)} %param.26) | copy-start | bytes 3076
